TPU v7x, 32 devices: a whole 2x2x4 slice. The times are simulated.
32 devices in a mesh: seq: 4 (over x, core), batch: 8 (over z, y).
Axes of the slice: x: 2, y: 2, z: 4, core: 2. Of those that a mesh axis runs over, the one named last changes fastest.
Arguments:
- tokens: bfloat16 [8, 2496, 512], P('batch', 'seq'), may hold values from -6 to 6
- doc_ids: int32 [8, 2496], P('batch'), may hold values from 0 to 6, as said below
- out_grad: bfloat16 [8, 832, 512], P('batch', 'seq'), may hold values from -6 to 6
- qkv_weight: float32 [3, 512, 512], P(None, ('seq', 'batch')), may hold values from -0.25 to 0.25
- qkv_first: float32 [3, 512, 512], P(None, ('seq', 'batch')), may hold values from -0.00030517578 to 0.00030517578
- qkv_second: float32 [3, 512, 512], P(None, ('seq', 'batch')), may hold values from 1.2699122e-10 to 2.0318596e-09
- proj_weight: float32 [512, 512], P(('seq', 'batch')), may hold values from -0.5 to 0.5
- proj_first: float32 [512, 512], P(('seq', 'batch')), may hold values from -0.00030517578 to 0.00030517578
- proj_second: float32 [512, 512], P(('seq', 'batch')), may hold values from 1.2699122e-10 to 2.0318596e-09
- up_weight: float32 [512, 2048], P(('seq', 'batch')), may hold values from -0.25 to 0.25
- up_first: float32 [512, 2048], P(('seq', 'batch')), may hold values from -0.00030517578 to 0.00030517578
- up_second: float32 [512, 2048], P(('seq', 'batch')), may hold values from 1.2699122e-10 to 2.0318596e-09
- down_weight: float32 [2048, 512], P(('seq', 'batch')), may hold values from -0.125 to 0.125
- down_first: float32 [2048, 512], P(('seq', 'batch')), may hold values from -0.00030517578 to 0.00030517578
- down_second: float32 [2048, 512], P(('seq', 'batch')), may hold values from 1.2699122e-10 to 2.0318596e-09
- pool_weight: float32 [1536, 512], P(('seq', 'batch')), may hold values from -0.15625 to 0.15625
- pool_first: float32 [1536, 512], P(('seq', 'batch')), may hold values from -0.00030517578 to 0.00030517578
- pool_second: float32 [1536, 512], P(('seq', 'batch')), may hold values from 1.2699122e-10 to 2.0318596e-09
- small_weight: float32 [5120], P(('seq', 'batch')), may hold values from -0.8 to 1.8
- small_first: float32 [5120], P(('seq', 'batch')), may hold values from -0.0012207031 to 0.0012207031
- small_second: float32 [5120], P(('seq', 'batch')), may hold values from 2.0318596e-09 to 3.2509753e-08
Outputs:
- short_out: bfloat16 [8, 832, 512], P('batch', 'seq')
- input_grad: float32 [8, 2496, 512], P('batch', 'seq')
- grad_norm: float32 [], replicated
- qkv_first_out: float32 [3, 512, 512], P(None, ('seq', 'batch'))
- qkv_second_out: float32 [3, 512, 512], P(None, ('seq', 'batch'))
- qkv_weight_out: float32 [3, 512, 512], P(None, ('seq', 'batch'))
- proj_first_out: float32 [512, 512], P(('seq', 'batch'))
- proj_second_out: float32 [512, 512], P(('seq', 'batch'))
- proj_weight_out: float32 [512, 512], P(('seq', 'batch'))
- up_first_out: float32 [512, 2048], P(('seq', 'batch'))
- up_second_out: float32 [512, 2048], P(('seq', 'batch'))
- up_weight_out: float32 [512, 2048], P(('seq', 'batch'))
- down_first_out: float32 [2048, 512], P(('seq', 'batch'))
- down_second_out: float32 [2048, 512], P(('seq', 'batch'))
- down_weight_out: float32 [2048, 512], P(('seq', 'batch'))
- pool_first_out: float32 [1536, 512], P(('seq', 'batch'))
- pool_second_out: float32 [1536, 512], P(('seq', 'batch'))
- pool_weight_out: float32 [1536, 512], P(('seq', 'batch'))
- small_first_out: float32 [5120], P(('seq', 'batch'))
- small_second_out: float32 [5120], P(('seq', 'batch'))
- small_weight_out: float32 [5120], P(('seq', 'batch'))
Inputs may be any that keep to these rules, and one draw needn't show every extreme that they name: `doc_ids`: in each sequence the ids start at 0, never fall, and rise by one at each document start; every sequence holds exactly seven documents, one of which begins within the first 624 positions and ends within the last 624 positions.
All inputs are finite; a program needn't handle non-finite values.
Results may differ from a plain program's by a relative error of at most 0.012.
Values may be sent and summed in bfloat16 or wider, within the bound.
A program may use at most 448 MiB of HBM per device.

v0:
```python
import math

import jax
import jax.numpy as jnp
from jax import lax
from jax.sharding import PartitionSpec as P

D = 512
HEAD_DIM = 64
STEP = 10


beta_one = 0.9
beta_two = 0.999
adam_eps = 1e-08
norm_eps = 1e-05
clip_norm = 1.0
rate_matrix = 0.05
rate_vector = 0.5
decay_weight = 0.1
masked_score = -1e30


def from_behind(block, axis, distance):
    devices = range(lax.axis_size(axis))
    route = [(i - distance, i) for i in devices if i - distance in devices]
    return lax.ppermute(block, axis, route)


def layer_norm(values, scale_gain, shift_vec):
    center = values - jnp.mean(values, axis=-1, keepdims=True)
    spread = jnp.mean(center * center, axis=-1, keepdims=True)
    return center * lax.rsqrt(spread + norm_eps) * scale_gain + shift_vec


def rotate(values, positions):
    half_dim = HEAD_DIM // 2
    head_view = values.reshape(values.shape[0], values.shape[1] // HEAD_DIM, HEAD_DIM)
    frequency = jnp.exp(-math.log(10000.0) * jnp.arange(half_dim, dtype=jnp.float32) / half_dim)
    angles = positions.astype(jnp.float32)[:, None] * frequency[None, :]
    cosine = jnp.cos(angles)[:, None, :]
    sine_part = jnp.sin(angles)[:, None, :]
    first_half = head_view[..., :half_dim]
    second_half = head_view[..., half_dim:]
    turned = jnp.concatenate(
        [
            first_half * cosine - second_half * sine_part,
            second_half * cosine + first_half * sine_part,
        ],
        axis=-1,
    )
    return turned.reshape(values.shape)


def outer_sum(left_side, right_side):
    return lax.dot_general(
        left_side, right_side, (((0,), (0,)), ((), ())), preferred_element_type=jnp.float32
    )


def times_transpose(left_side, right_side):
    return lax.dot_general(
        left_side, right_side, (((1,), (1,)), ((), ())), preferred_element_type=jnp.float32
    )


def split_heads(values):
    return values.reshape(values.shape[0], values.shape[1] // HEAD_DIM, HEAD_DIM)


def block_scores(query_heads, key_heads, query_pos, key_pos, query_doc, key_doc):
    raw_scores = jnp.einsum(
        "qhd,khd->hqk", query_heads, key_heads, preferred_element_type=jnp.float32
    ) * HEAD_DIM ** (-0.5)
    allowed = (key_pos[None, :] <= query_pos[:, None]) & (key_doc[None, :] == query_doc[:, None])
    return jnp.where(allowed[None], raw_scores, masked_score)


def adam_update(gradient, first_moment, second_moment, weight, clip_scale, step_rate, decay_rate):
    clipped = gradient * clip_scale
    first_new = beta_one * first_moment + (1.0 - beta_one) * clipped
    second_new = beta_two * second_moment + (1.0 - beta_two) * clipped * clipped
    first_hat = first_new / (1.0 - beta_one**STEP)
    second_hat = second_new / (1.0 - beta_two**STEP)
    weight_new = weight - step_rate * (
        first_hat / (jnp.sqrt(second_hat) + adam_eps) + decay_rate * weight
    )
    return (first_new, second_new, weight_new)


def local(
    tokens,
    doc_ids,
    out_grad,
    qkv_weight,
    qkv_first,
    qkv_second,
    proj_weight,
    proj_first,
    proj_second,
    up_weight,
    up_first,
    up_second,
    down_weight,
    down_first,
    down_second,
    pool_weight,
    pool_first,
    pool_second,
    small_weight,
    small_first,
    small_second,
):
    block_rows = tokens.shape[1]
    model_width = tokens.shape[2]
    seq_count = lax.axis_size("seq")
    my_block = lax.axis_index("seq")
    whole_qkv, whole_proj, whole_up, whole_down, whole_pool, whole_small = (
        lax.all_gather(qkv_weight.astype(jnp.bfloat16), ("seq", "batch"), axis=1, tiled=True),
        lax.all_gather(proj_weight.astype(jnp.bfloat16), ("seq", "batch"), axis=0, tiled=True),
        lax.all_gather(up_weight.astype(jnp.bfloat16), ("seq", "batch"), axis=0, tiled=True),
        lax.all_gather(down_weight.astype(jnp.bfloat16), ("seq", "batch"), axis=0, tiled=True),
        lax.all_gather(pool_weight.astype(jnp.bfloat16), ("seq", "batch"), axis=0, tiled=True),
        lax.all_gather(small_weight.astype(jnp.bfloat16), ("seq", "batch"), axis=0, tiled=True),
    )
    small_used = whole_small.astype(jnp.float32)
    gain_first = small_used[0:D]
    shift_first = small_used[D : 2 * D]
    gain_second = small_used[2 * D : 3 * D]
    shift_second = small_used[3 * D : 4 * D]
    bias_down = small_used[4 * D : 5 * D]
    bias_pool = small_used[5 * D : 6 * D]
    bias_up = small_used[6 * D :]
    inputs = tokens[0].astype(jnp.float32)
    doc_row = doc_ids[0]
    first_row = my_block * block_rows
    positions = first_row + jnp.arange(block_rows, dtype=jnp.int32)
    doc_mine = lax.dynamic_slice_in_dim(doc_row, first_row, block_rows)
    normed, first_pull = jax.vjp(layer_norm, inputs, gain_first, shift_first)
    normed_low = normed.astype(jnp.bfloat16)
    projected = jnp.einsum("td,cde->cte", normed_low, whole_qkv, preferred_element_type=jnp.float32)
    queries_rot, query_pull = jax.vjp(lambda values: rotate(values, positions), projected[0])
    keys_rot, key_pull = jax.vjp(lambda values: rotate(values, positions), projected[1])
    query_low = queries_rot.astype(jnp.bfloat16)
    key_low = keys_rot.astype(jnp.bfloat16)
    value_low = projected[2].astype(jnp.bfloat16)
    keys_all, values_all = (
        lax.all_gather(key_low, "seq", axis=0, tiled=True),
        lax.all_gather(value_low, "seq", axis=0, tiled=True),
    )
    query_heads = split_heads(query_low)
    head_count = query_heads.shape[1]
    zeros_head_rows = jnp.zeros((head_count, block_rows), jnp.float32)
    zeros_heads = jnp.zeros((block_rows, head_count, HEAD_DIM), jnp.float32)

    def scores_of(number):
        start_row = number * block_rows
        key_heads = split_heads(keys_all[start_row : start_row + block_rows])
        value_heads = split_heads(values_all[start_row : start_row + block_rows])
        key_pos = start_row + jnp.arange(block_rows, dtype=jnp.int32)
        key_doc = doc_row[start_row : start_row + block_rows]
        scores = block_scores(query_heads, key_heads, positions, key_pos, doc_mine, key_doc)
        return (scores, key_heads, value_heads)

    running_max = jnp.full((head_count, block_rows), masked_score, jnp.float32)
    running_sum = zeros_head_rows
    for number in range(seq_count):

        def block_stats(number=number):
            scores = scores_of(number)[0]
            block_max = jnp.max(scores, axis=-1)
            return (block_max, jnp.sum(jnp.exp(scores - block_max[..., None]), axis=-1))

        block_max, block_sum = block_stats()
        new_max = jnp.maximum(running_max, block_max)
        running_sum = running_sum * jnp.exp(running_max - new_max) + block_sum * jnp.exp(
            block_max - new_max
        )
        running_max = new_max
    log_total = running_max + jnp.log(running_sum)
    attended = zeros_heads
    for number in range(seq_count):

        def block_output(number=number):
            scores, key_heads, value_heads = scores_of(number)
            soft_probs = jnp.exp(scores - log_total[..., None]).astype(jnp.bfloat16)
            return jnp.einsum(
                "hqk,khd->qhd", soft_probs, value_heads, preferred_element_type=jnp.float32
            )

        attended = attended + block_output()
    attended_low = attended.reshape(block_rows, model_width).astype(jnp.bfloat16)
    h_one = inputs + jnp.dot(attended_low, whole_proj, preferred_element_type=jnp.float32)
    normed_two, second_pull = jax.vjp(layer_norm, h_one, gain_second, shift_second)
    normed_two_low = normed_two.astype(jnp.bfloat16)
    hidden_pre = jnp.dot(normed_two_low, whole_up, preferred_element_type=jnp.float32) + bias_up
    activated, gelu_pull = jax.vjp(jax.nn.gelu, hidden_pre)
    act_low = activated.astype(jnp.bfloat16)
    h_two = h_one + jnp.dot(act_low, whole_down, preferred_element_type=jnp.float32) + bias_down
    h_two_low = h_two.astype(jnp.bfloat16)
    prev_rows = from_behind(h_two_low[block_rows - 2 :], "seq", 1)
    shifted = jnp.concatenate([prev_rows, h_two_low[: block_rows - 2]], axis=0)
    grouped = shifted.reshape(block_rows // 3, 3 * model_width)
    short_rows = (
        jnp.dot(grouped, whole_pool, preferred_element_type=jnp.float32) + bias_pool
    ).astype(jnp.bfloat16)
    out_rows = out_grad[0]
    grad_pool = outer_sum(grouped, out_rows)
    grad_bias_pool = jnp.sum(out_rows.astype(jnp.float32), axis=0)
    spread_rows = times_transpose(out_rows, whole_pool).reshape(block_rows, model_width)
    returned = from_behind(spread_rows[:2], "seq", -1)
    grad_h_two = jnp.concatenate([spread_rows[2:], returned], axis=0)
    grad_branch = grad_h_two.astype(jnp.bfloat16)
    grad_down = outer_sum(act_low, grad_branch)
    grad_bias_down = jnp.sum(grad_branch.astype(jnp.float32), axis=0)
    grad_act = times_transpose(grad_branch, whole_down)
    grad_hidden = gelu_pull(grad_act)[0].astype(jnp.bfloat16)
    grad_up = outer_sum(normed_two_low, grad_hidden)
    grad_bias_up = jnp.sum(grad_hidden.astype(jnp.float32), axis=0)
    grad_normed_two = times_transpose(grad_hidden, whole_up)
    back_h_one, grad_gain_second, grad_shift_second = second_pull(grad_normed_two)
    grad_h_one = grad_h_two + back_h_one
    grad_attn = grad_h_one.astype(jnp.bfloat16)
    grad_proj = outer_sum(attended_low, grad_attn)
    grad_attended = times_transpose(grad_attn, whole_proj).astype(jnp.bfloat16)
    grad_heads = split_heads(grad_attended)
    row_delta = zeros_head_rows
    value_terms = []
    for number in range(seq_count):

        def block_first(number=number):
            scores, key_heads, value_heads = scores_of(number)
            soft_probs = jnp.exp(scores - log_total[..., None])
            grad_probs = jnp.einsum(
                "qhd,khd->hqk", grad_heads, value_heads, preferred_element_type=jnp.float32
            )
            part_delta = jnp.sum(soft_probs * grad_probs, axis=-1)
            value_grad = jnp.einsum(
                "hqk,qhd->khd",
                soft_probs.astype(jnp.bfloat16),
                grad_heads,
                preferred_element_type=jnp.float32,
            )
            return (part_delta, value_grad.reshape(block_rows, model_width))

        part_delta, value_grad = block_first()
        row_delta = row_delta + part_delta
        value_terms.append(value_grad)
    grad_query = zeros_heads
    key_terms = []
    for number in range(seq_count):

        def block_second(number=number):
            scores, key_heads, value_heads = scores_of(number)
            soft_probs = jnp.exp(scores - log_total[..., None])
            grad_probs = jnp.einsum(
                "qhd,khd->hqk", grad_heads, value_heads, preferred_element_type=jnp.float32
            )
            grad_scores = (soft_probs * (grad_probs - row_delta[..., None])).astype(jnp.bfloat16)
            query_part = jnp.einsum(
                "hqk,khd->qhd", grad_scores, key_heads, preferred_element_type=jnp.float32
            )
            key_part = jnp.einsum(
                "hqk,qhd->khd", grad_scores, query_heads, preferred_element_type=jnp.float32
            )
            return (query_part, key_part.reshape(block_rows, model_width))

        query_part, key_part = block_second()
        grad_query = grad_query + query_part
        key_terms.append(key_part)
    head_scale = HEAD_DIM ** (-0.5)
    grad_keys, grad_values = (
        lax.psum_scatter(
            (jnp.concatenate(key_terms, axis=0) * head_scale).astype(jnp.bfloat16),
            "seq",
            scatter_dimension=0,
            tiled=True,
        ).astype(jnp.float32),
        lax.psum_scatter(
            jnp.concatenate(value_terms, axis=0).astype(jnp.bfloat16),
            "seq",
            scatter_dimension=0,
            tiled=True,
        ).astype(jnp.float32),
    )
    grad_q_pre = query_pull(grad_query.reshape(block_rows, model_width) * head_scale)[0].astype(
        jnp.bfloat16
    )
    grad_k_pre = key_pull(grad_keys)[0].astype(jnp.bfloat16)
    grad_v_pre = grad_values.astype(jnp.bfloat16)
    stacked = jnp.stack([grad_q_pre, grad_k_pre, grad_v_pre])
    grad_qkv = jnp.einsum("td,cte->cde", normed_low, stacked, preferred_element_type=jnp.float32)
    grad_normed = jnp.einsum("cte,cde->td", stacked, whole_qkv, preferred_element_type=jnp.float32)
    back_inputs, grad_gain_first, grad_shift_first = first_pull(grad_normed)
    input_grad = (grad_h_one + back_inputs)[None]
    grad_small = jnp.concatenate(
        [
            grad_gain_first,
            grad_shift_first,
            grad_gain_second,
            grad_shift_second,
            grad_bias_down,
            grad_bias_pool,
            grad_bias_up,
        ]
    )
    all_grads = (grad_qkv, grad_proj, grad_up, grad_down, grad_pool, grad_small)
    shards = (
        lax.psum_scatter(all_grads[0], ("seq", "batch"), scatter_dimension=1, tiled=True),
        lax.psum_scatter(all_grads[1], ("seq", "batch"), scatter_dimension=0, tiled=True),
        lax.psum_scatter(all_grads[2], ("seq", "batch"), scatter_dimension=0, tiled=True),
        lax.psum_scatter(all_grads[3], ("seq", "batch"), scatter_dimension=0, tiled=True),
        lax.psum_scatter(all_grads[4], ("seq", "batch"), scatter_dimension=0, tiled=True),
        lax.psum_scatter(all_grads[5], ("seq", "batch"), scatter_dimension=0, tiled=True),
    )
    local_squares = sum((jnp.sum(portion * portion) for portion in shards))
    grad_norm = jnp.sqrt(lax.psum(local_squares, ("seq", "batch")))
    clip_scale = clip_norm / jnp.maximum(grad_norm, clip_norm)
    masters = (qkv_weight, proj_weight, up_weight, down_weight, pool_weight, small_weight)
    firsts = (qkv_first, proj_first, up_first, down_first, pool_first, small_first)
    seconds = (qkv_second, proj_second, up_second, down_second, pool_second, small_second)
    new_states = []
    for index_kind in range(6):
        step_rate = rate_vector if index_kind == 5 else rate_matrix
        decay_rate = 0.0 if index_kind == 5 else decay_weight
        new_states.append(
            adam_update(
                shards[index_kind],
                firsts[index_kind],
                seconds[index_kind],
                masters[index_kind],
                clip_scale,
                step_rate,
                decay_rate,
            )
        )
    return (
        short_rows[None],
        input_grad,
        grad_norm,
        new_states[0][0],
        new_states[0][1],
        new_states[0][2],
        new_states[1][0],
        new_states[1][1],
        new_states[1][2],
        new_states[2][0],
        new_states[2][1],
        new_states[2][2],
        new_states[3][0],
        new_states[3][1],
        new_states[3][2],
        new_states[4][0],
        new_states[4][1],
        new_states[4][2],
        new_states[5][0],
        new_states[5][1],
        new_states[5][2],
    )


def solution(mesh):
    in_specs = (
        P("batch", "seq", None),
        P("batch", None),
        P("batch", "seq", None),
        P(None, ("seq", "batch"), None),
        P(None, ("seq", "batch"), None),
        P(None, ("seq", "batch"), None),
        P(("seq", "batch"), None),
        P(("seq", "batch"), None),
        P(("seq", "batch"), None),
        P(("seq", "batch"), None),
        P(("seq", "batch"), None),
        P(("seq", "batch"), None),
        P(("seq", "batch"), None),
        P(("seq", "batch"), None),
        P(("seq", "batch"), None),
        P(("seq", "batch"), None),
        P(("seq", "batch"), None),
        P(("seq", "batch"), None),
        P(("seq", "batch")),
        P(("seq", "batch")),
        P(("seq", "batch")),
    )
    out_specs = (
        P("batch", "seq", None),
        P("batch", "seq", None),
        P(),
        P(None, ("seq", "batch"), None),
        P(None, ("seq", "batch"), None),
        P(None, ("seq", "batch"), None),
        P(("seq", "batch"), None),
        P(("seq", "batch"), None),
        P(("seq", "batch"), None),
        P(("seq", "batch"), None),
        P(("seq", "batch"), None),
        P(("seq", "batch"), None),
        P(("seq", "batch"), None),
        P(("seq", "batch"), None),
        P(("seq", "batch"), None),
        P(("seq", "batch"), None),
        P(("seq", "batch"), None),
        P(("seq", "batch"), None),
        P(("seq", "batch")),
        P(("seq", "batch")),
        P(("seq", "batch")),
    )
    return jax.shard_map(local, mesh=mesh, in_specs=in_specs, out_specs=out_specs, check_vma=False)
```

profile of v0, /device:TPU:12, one launch (start us, length us, event | category | flops | bytes accessed | tf_op | source)
XLA Modules:
  0.0 1301.3 jit_solution(726679316228760924)
XLA Ops:
  11.3 41.6 %all-reduce.4 = bf16[5120]{0:T(1024)(128)(2,1)S(1)} all-reduce(bf16[5120]{0:T(1024)(128)(2,1)S(1)} %dynamic-update-slice), channel_id=1, replica_groups=mesh['seq'=4,'batch'=8] {'seq','batch'}, use_global_device_ids=true, to_apply=%add.4 | all-reduce | flops 5120 | bytes 20480
  56.2 10.7 all-gather.8.cloned.1.call-done
  84.9 39.4 %all-gather.16.cloned.1.call-done = bf16[1536,512]{1,0:T(8,128)(2,1)} async-done(((bf16[48,512]{1,0:T(8,128)(2,1)}), bf16[1536,512]{1,0:T(8,128)(2,1)}) %all-gather.16.cloned.1.call-update) | async-done | bytes 1572880 | tf_op jit(solution)/shard_map/all_gather | solution.py:123
  132.0 71.2 %all_gather.28 = bf16[512,512]{1,0:T(8,128)(2,1)} all-gather(bf16[16,512]{1,0:T(8,128)(2,1)S(1)} %convert_element_type.167), channel_id=1, replica_groups=mesh['seq'=4,'batch'=8] {'seq','batch'}, dimensions={0}, use_global_device_ids=true | all-gather | bytes 540672 | tf_op jit(solution)/shard_map/all_gather | solution.py:120
  234.2 8.5 fusion.2
  242.7 19.6 %exponential_reduce_fusion.1 = f32[8,624]{1,0:T(8,128)S(1)} fusion(f32[8,624,624]{1,2,0:T(8,128)} %get-tuple-element.169, f32[8,624]{1,0:T(8,128)S(1)} %get-tuple-element.168, pred[624,624]{0,1:T(8,128)(4,1)S(1)} %get-tuple-element.159), kind=kLoop, calls=%fused_computation.13 | loop fusion | flops 12455040 | bytes 12889344 | tf_op jit(solution)/shard_map/reduce_sum | solution.py:172
  268.3 7.4 exponential_reduce_fusion
  281.8 7.3 exponential_reduce_fusion.2
  295.1 9.6 convolution_add_fusion.5
  322.9 7.7 convert_reduce_fusion
  338.1 7.9 fusion.117
  359.1 36.0 %multiply_reduce_fusion.2 = (f32[8,624]{1,0:T(8,128)S(1)}, f32[8,624]{1,0:T(8,128)S(1)}, f32[8,624]{1,0:T(8,128)S(1)}, f32[8,624]{1,0:T(8,128)S(1)}, f32[8,624,624]{1,2,0:T(8,128)}) fusion(f32[8,624,624]{1,2,0:T(8,128)} %get-tuple-element.171, f32[8,624]{1,0:T(8,128)S(1)} %fusion.60, pred[624,624]{0,1:T(8,128)(4,1)S(1)} %copy-done.11, ...), kind=kOutput, calls=%fused_computation.6 | convolution fusion | flops 461001216 | bytes 102615552 | tf_op jit(solution)/shard_map/qhd,khd->hqk/dot_general | solution.py:234
  395.0 43.8 %multiply_convert_fusion = (bf16[8,624,624]{1,2,0:T(8,128)(2,1)}, bf16[8,624,624]{1,2,0:T(8,128)(2,1)}, bf16[8,624,624]{1,2,0:T(8,128)(2,1)}, bf16[8,624,624]{1,2,0:T(8,128)(2,1)}) fusion(f32[8,624,624]{1,2,0:T(8,128)} %fusion.117, f32[8,624,624]{1,2,0:T(8,128)} %get-tuple-element.167, f32[8,624]{1,0:T(8,128)S(1)} %add_add_fusion.3, f32[8,624]{1,0:T(8,128)S(1)} %fusion.60, ...), kind=kLoop, calls=%fused_computation | loop fusion | flops 74760192 | bytes 126197760 | tf_op jit(solution)/shard_map/convert_element_type | solution.py:259
  473.9 8.7 convolution_convert_fusion
  484.8 9.2 convolution_convert_fusion.1
  496.4 8.7 convolution_convert_fusion.2
  507.4 9.2 convolution_convert_fusion.3
  588.0 102.8 %reduce-scatter.11.cloned.1.call-done = f32[16,512]{1,0:T(8,128)} async-done(((f32[512,512]{1,0:T(8,128)}), f32[16,512]{1,0:T(8,128)}) %reduce-scatter.11.cloned.1.call-update) | async-done | bytes 32784 | tf_op jit(solution)/shard_map/reduce_scatter | solution.py:310
  692.2 109.2 %reduce-scatter.17.cloned.1.call-done = f32[48,512]{1,0:T(8,128)} async-done(((f32[1536,512]{1,0:T(8,128)}), f32[48,512]{1,0:T(8,128)}) %reduce-scatter.17.cloned.1.call-update) | async-done | bytes 98320 | tf_op jit(solution)/shard_map/reduce_scatter | solution.py:313
  816.1 40.8 %all-reduce.6 = f32[5120]{0:T(1024)S(1)} all-reduce(f32[5120]{0:T(1024)} %constant_dynamic-update-slice_fusion), channel_id=10, replica_groups=mesh['seq'=4,'batch'=8] {'seq','batch'}, use_global_device_ids=true, to_apply=%region_39.40.clone | all-reduce | flops 5120 | bytes 40960
  858.9 89.4 %all-reduce.9.cloned.1.call-done = f32[3,512,512]{2,0,1:T(4,128)} async-done(((f32[3,512,512]{2,0,1:T(4,128)}), f32[3,512,512]{2,0,1:T(4,128)}) %all-reduce.9.cloned.1.call-update) | async-done | bytes 3145744
  951.8 136.8 %reduce-scatter.13.cloned.1.call-done = f32[16,2048]{1,0:T(8,128)} async-done(((f32[512,2048]{1,0:T(8,128)}), f32[16,2048]{1,0:T(8,128)}) %reduce-scatter.13.cloned.1.call-update) | async-done | bytes 131088 | tf_op jit(solution)/shard_map/reduce_scatter | solution.py:311
  1090.8 141.8 %reduce-scatter.15.cloned.1.call-done = f32[64,512]{1,0:T(8,128)} async-done(((f32[2048,512]{1,0:T(8,128)}), f32[64,512]{1,0:T(8,128)}) %reduce-scatter.15.cloned.1.call-update) | async-done | bytes 131088 | tf_op jit(solution)/shard_map/reduce_scatter | solution.py:312
  1238.3 44.3 %psum.7 = f32[]{:T(128)} all-reduce(f32[]{:T(128)S(6)} %add.386), channel_id=1, replica_groups=mesh['seq'=4,'batch'=8] {'seq','batch'}, use_global_device_ids=true, to_apply=%region_41.42 | all-reduce | flops 1 | bytes 8 | tf_op jit(solution)/shard_map/psum | solution.py:317
  (340 shorter events, 268.2 us)
Async XLA Ops:
  7.2 59.8 %all-gather.8.cloned.1.call-start = ((), (), s32[]{:S(2)}) async-start(), calls=%async_computation.6 | async-start | bytes 1622016 | tf_op jit(solution)/shard_map/all_gather | solution.py:119
  8.8 115.6 %all-gather.16.cloned.1.call-start = ((), (), s32[]{:S(2)}) async-start(), calls=%async_computation.10 | async-start | bytes 1622016 | tf_op jit(solution)/shard_map/all_gather | solution.py:123
  10.4 196.9 %all-gather.18.cloned.1.call-start = ((), (), s32[]{:S(2)}) async-start(), calls=%async_computation.16 | async-start | bytes 3194880 | tf_op jit(solution)/shard_map/all_gather | solution.py:149
  56.2 261.2 %copy-start.54 = (f32[512]{0:T(512)}, f32[512]{0:T(512)S(1)}, u32[]{:S(2)}) copy-start(f32[512]{0:T(512)S(1)} %get-tuple-element.154) | copy-start | bytes 6148
  56.2 276.8 %copy-start.50 = (f32[512]{0:T(512)}, f32[512]{0:T(512)S(1)}, u32[]{:S(2)}) copy-start(f32[512]{0:T(512)S(1)} %get-tuple-element.153) | copy-start | bytes 6148
  72.6 145.2 %all-gather.10.cloned.1.call-start = ((), (), s32[]{:S(2)}) async-start(), calls=%async_computation.7 | async-start | bytes 3194880 | tf_op jit(solution)/shard_map/all_gather | solution.py:148
  79.9 237.5 %all-gather.12.cloned.1.call-start = ((), (), s32[]{:S(2)}) async-start(), calls=%async_computation.8 | async-start | bytes 2162688 | tf_op jit(solution)/shard_map/all_gather | solution.py:121
  81.5 241.4 %all-gather.14.cloned.1.call-start = ((), (), s32[]{:S(2)}) async-start(), calls=%async_computation.9 | async-start | bytes 2162688 | tf_op jit(solution)/shard_map/all_gather | solution.py:122
  83.1 465.1 %reduce-scatter.19.cloned.1.call-start = ((), (), s32[]{:S(2)}) async-start(), calls=%async_computation.17 | async-start | bytes 3194880
  84.9 204.3 %copy-start.8 = (pred[624,624]{0,1:T(8,128)(4,1)}, pred[624,624]{0,1:T(8,128)(4,1)S(1)}, u32[]{:S(2)}) copy-start(pred[624,624]{0,1:T(8,128)(4,1)S(1)} %get-tuple-element.161) | copy-start | bytes 1168132
  84.9 210.2 %copy-start.10 = (pred[624,624]{0,1:T(8,128)(4,1)}, pred[624,624]{0,1:T(8,128)(4,1)S(1)}, u32[]{:S(2)}) copy-start(pred[624,624]{0,1:T(8,128)(4,1)S(1)} %get-tuple-element.158) | copy-start | bytes 1168132
  84.9 219.8 %copy-start.12 = (pred[624,624]{0,1:T(8,128)(4,1)}, pred[624,624]{0,1:T(8,128)(4,1)S(1)}, u32[]{:S(2)}) copy-start(pred[624,624]{0,1:T(8,128)(4,1)S(1)} %get-tuple-element.159) | copy-start | bytes 1168132
  84.9 225.8 %copy-start.14 = (pred[624,624]{0,1:T(8,128)(4,1)}, pred[624,624]{0,1:T(8,128)(4,1)S(1)}, u32[]{:S(2)}) copy-start(pred[624,624]{0,1:T(8,128)(4,1)S(1)} %get-tuple-element.160) | copy-start | bytes 1168132
  130.7 74.0 %collective-permute-start.1 = (f32[2,512]{1,0:T(2,128)S(1)}, f32[2,512]{1,0:T(2,128)S(1)}, u32[]{:S(2)}, u32[]{:S(2)}) collective-permute-start(f32[2,512]{1,0:T(2,128)S(1)} %slice.198), channel_id=1, source_target_pairs={{8,0},{16,8},{24,16},{9,1},{17,9},{25,17},{10,2},{18,10},{26,18},{... | collective-permute-start | bytes 12296 | tf_op jit(solution)/shard_map/ppermute | solution.py:27
  473.6 86.3 %reduce-scatter.9.cloned.1.call-start = ((), (), s32[]{:S(2)}) async-start(), calls=%async_computation.11 | async-start | bytes 3194880 | tf_op jit(solution)/shard_map/reduce_scatter | solution.py:279
  521.7 169.1 %reduce-scatter.11.cloned.1.call-start = ((), (), s32[]{:S(2)}) async-start(), calls=%async_computation.12 | async-start | bytes 1081344 | tf_op jit(solution)/shard_map/reduce_scatter | solution.py:310
  523.3 278.0 %reduce-scatter.17.cloned.1.call-start = ((), (), s32[]{:S(2)}) async-start(), calls=%async_computation.15 | async-start | bytes 3244032 | tf_op jit(solution)/shard_map/reduce_scatter | solution.py:313
  528.6 2.1 collective-permute-start
  535.4 413.0 %all-reduce.9.cloned.1.call-start = ((), (), s32[]{:S(2)}) async-start(), calls=%async_computation.18 | async-start | bytes 8388608
  569.8 518.8 %reduce-scatter.13.cloned.1.call-start = ((), (), s32[]{:S(2)}) async-start(), calls=%async_computation.13 | async-start | bytes 4325376 | tf_op jit(solution)/shard_map/reduce_scatter | solution.py:311
  576.2 656.4 %reduce-scatter.15.cloned.1.call-start = ((), (), s32[]{:S(2)}) async-start(), calls=%async_computation.14 | async-start | bytes 4325376 | tf_op jit(solution)/shard_map/reduce_scatter | solution.py:312
  806.3 478.4 %copy-start.43 = (f32[3,16,512]{2,1,0:T(8,128)S(1)}, f32[3,16,512]{2,1,0:T(8,128)}, u32[]{:S(2)}) copy-start(f32[3,16,512]{2,1,0:T(8,128)} %param.24) | copy-start | bytes 294916
  806.3 481.6 %copy-start.44 = (f32[48,512]{1,0:T(8,128)S(1)}, f32[48,512]{1,0:T(8,128)}, u32[]{:S(2)}) copy-start(f32[48,512]{1,0:T(8,128)} %param.36) | copy-start | bytes 294916
  807.6 482.1 %copy-start.42 = (f32[16,2048]{1,0:T(8,128)S(1)}, f32[16,2048]{1,0:T(8,128)}, u32[]{:S(2)}) copy-start(f32[16,2048]{1,0:T(8,128)} %param.30) | copy-start | bytes 393220
  (77 other events, 642.5 us)
Sparse Core Ops, SparseCore 0:
  11.6 55.2 all-gather.7
  70.4 53.8 all-gather.15
  125.9 25.0 all-gather.17
  152.5 25.1 all-gather.9
  181.1 55.6 all-gather.11
  240.2 55.3 all-gather.13
  473.8 37.5 reduce-scatter.18
  521.8 37.8 reduce-scatter.8
  562.6 128.1 reduce-scatter.10
  697.0 104.3 reduce-scatter.16
  807.8 140.4 all-reduce.8
  950.6 138.0 reduce-scatter.12
  1091.0 141.5 reduce-scatter.14
where the time goes:
time: 1310 us; the launch traced here: 1300 us
  waiting for transfers between devices  631 us (48%)
  matrix products  230 us (18%)
  blocking collectives  198 us (15%)
  other arithmetic  134 us (10%)
  local copies, waits for them, and re-layouts  83.9 us (6%)
  between operations  21 us (2%)
    reduce_scatter x1, waiting for transfers between devices, local(): lax.psum_scatter(all_grads[3], ('seq', 'batch'), scatter_dimension=0, til...  142 us
    reduce_scatter x1, waiting for transfers between devices, local(): lax.psum_scatter(all_grads[2], ('seq', 'batch'), scatter_dimension=0, til...  137 us
    reduce_scatter x1, waiting for transfers between devices, local(): lax.psum_scatter(all_grads[4], ('seq', 'batch'), scatter_dimension=0, til...  109 us
    reduce_scatter x1, waiting for transfers between devices, local(): lax.psum_scatter(all_grads[1], ('seq', 'batch'), scatter_dimension=0, til...  103 us
    unnamed x15, waiting for transfers between devices  89.7 us
    unnamed x2, blocking collectives  82.4 us
    all_gather x1, blocking collectives, local(): lax.all_gather(proj_weight.astype(jnp.bfloat16), ('seq', 'batch'), axis=0...  71.2 us
    dot_general x3, matrix products, block_first(): jnp.einsum('qhd,khd->hqk', grad_heads, value_heads, preferred_element_typ...  50.4 us
  transfers between devices with their start and end apart: 15, of which 8 were waited for; matrix products, arithmetic and copies ran while one was open for 21% of the time, Pallas kernels for 0%

commit v1 on v0

--- a/solution.py
+++ b/solution.py
@@ -3,6 +3,8 @@
 import jax
 import jax.numpy as jnp
 from jax import lax
+from jax.experimental import pallas as pl
+from jax.experimental.pallas import tpu as pltpu
 from jax.sharding import PartitionSpec as P
 
 D = 512
@@ -359,6 +361,925 @@
     )
 
 
+MESH = pl.DeviceIdType.MESH
+BF = jnp.bfloat16
+F32 = jnp.float32
+WIDE = 128
+LOG2E = math.log2(math.e)
+NN = (((1,), (0,)), ((), ()))
+NT = (((1,), (1,)), ((), ()))
+TN = (((0,), (0,)), ((), ()))
+VMEM_LIMIT = 60 * 2**20
+ARRAYS = 5
+GELU_C = math.sqrt(2.0 / math.pi)
+
+
+def dot(a, b, dims=NN):
+    return lax.dot_general(a, b, dims, preferred_element_type=F32)
+
+
+def grid_of(mesh):
+    seq, batch = mesh.shape["seq"], mesh.shape["batch"]
+    ny = 2 if batch % 2 == 0 else 1
+    return seq // 2, batch // ny, ny
+
+
+def fits(mesh):
+    seq, batch = mesh.shape["seq"], mesh.shape["batch"]
+    return seq == 4 and batch % 2 == 0 and D % (seq * batch * 16) == 0
+
+
+class Where:
+    def __init__(self, nx, nz, ny):
+        self.nx, self.nz, self.ny = nx, nz, ny
+        seq, batch = lax.axis_index("seq"), lax.axis_index("batch")
+        self.seq = seq
+        self.batch = batch
+        self.x, self.c = lax.div(seq, 2), lax.rem(seq, 2)
+        self.z, self.y = lax.div(batch, ny), lax.rem(batch, ny)
+        self.xo, self.co, self.yo = 1 - self.x, 1 - self.c, 1 - self.y
+
+    def dev(self, x=None, c=None, z=None, y=None):
+        x = self.x if x is None else x
+        c = self.c if c is None else c
+        z = self.z if z is None else z
+        y = self.y if y is None else y
+        return (x * 2 + c, z * self.ny + y)
+
+    def z_at(self, step):
+        return lax.rem(self.z + step, self.nz)
+
+    def seq_at(self, step):
+        return lax.rem(self.seq + step, 2 * self.nx)
+
+    def partner(self, stage):
+        return {
+            "x": self.dev(x=self.xo),
+            "c": self.dev(c=self.co),
+            "y": self.dev(y=self.yo),
+        }[stage]
+
+    def axis_peers(self):
+        peers = [self.partner(s) for s in "xcy"]
+        return peers + [self.dev(z=self.z_at(k)) for k in range(1, self.nz)]
+
+    def seq_peers(self):
+        return [(self.seq_at(k), self.batch) for k in range(1, 2 * self.nx)]
+
+
+def greet(peers):
+    barrier = pltpu.get_barrier_semaphore()
+    for peer in peers:
+        pl.semaphore_signal(barrier, inc=1, device_id=peer, device_id_type=MESH)
+    return barrier
+
+
+def remote(src, dst, send, recv, peer):
+    return pltpu.make_async_remote_copy(
+        src, dst, send, recv, device_id=peer, device_id_type=MESH
+    )
+
+
+class Gather:
+    ORDERS = ("zxyc", "zyxc", "zyxc", "zxyc", "zyxc")
+
+    def __init__(self, w, fulls, small, small_in, send, recv):
+        self.w, self.fulls, self.send, self.recv = w, fulls, send, recv
+        self.small, self.small_in = small, small_in
+        self.copies = {}
+
+    def view(self, a, stage):
+        order = self.ORDERS[a]
+        done = order[: order.index(stage)]
+        w = self.w
+        pick = [
+            slice(None) if name in done else own
+            for name, own in (("x", w.x), ("c", w.c), ("z", w.z), ("y", w.y))
+        ]
+        return self.fulls[a].at[pick[0], pick[1], pick[2], pick[3]]
+
+    def start(self, a, index):
+        w = self.w
+        stage = self.ORDERS[a][index]
+        block = self.view(a, stage)
+        made = []
+        if stage == "z":
+            for k in range(1, w.nz):
+                made.append(
+                    remote(block, block, self.send.at[a, k - 1], self.recv.at[a, k - 1],
+                           w.dev(z=w.z_at(k)))
+                )
+        else:
+            slot = w.nz - 1 + "xyc".index(stage)
+            made.append(
+                remote(block, block, self.send.at[a, slot], self.recv.at[a, slot],
+                       w.partner(stage))
+            )
+        for copy in made:
+            copy.start()
+        self.copies[a, index] = made
+
+    def wait(self, a, index):
+        for copy in self.copies[a, index]:
+            copy.wait_recv()
+
+    def finish(self):
+        for made in self.copies.values():
+            for copy in made:
+                copy.wait_send()
+
+
+def norm_stats(values):
+    center = values - jnp.mean(values, axis=-1, keepdims=True)
+    spread = jnp.mean(center * center, axis=-1, keepdims=True)
+    scale = lax.rsqrt(spread + norm_eps)
+    return center * scale, scale
+
+
+def norm_back(grad, unit, scale, gain):
+    inner = grad * gain
+    mean_one = jnp.mean(inner, axis=-1, keepdims=True)
+    mean_two = jnp.mean(inner * unit, axis=-1, keepdims=True)
+    back = scale * (inner - mean_one - unit * mean_two)
+    return back, jnp.sum(grad * unit, axis=0, keepdims=True), jnp.sum(grad, axis=0, keepdims=True)
+
+
+def swap_halves(values):
+    lane = lax.broadcasted_iota(jnp.int32, values.shape, 1)
+    return jnp.where(
+        lax.rem(lane, HEAD_DIM) < HEAD_DIM // 2,
+        pltpu.roll(values, WIDE - HEAD_DIM // 2, 1),
+        pltpu.roll(values, HEAD_DIM // 2, 1),
+    )
+
+
+def start_kernel(nx, nz, ny, tokens, qkv_w, proj_w, up_w, down_w, pool_w, small_in, turn,
+                 g_qkv, g_proj, g_up, g_down, g_pool, small, qkv_all,
+                 chunk, small_got, send, recv, send_small, recv_small, send_x, recv_x):
+    w = Where(nx, nz, ny)
+    rows = tokens.shape[0]
+    peers = w.axis_peers() + [w.dev(x=w.xo, c=w.co)]
+    barrier = greet(peers)
+    shards = (qkv_w, proj_w, up_w, down_w, pool_w)
+    fulls = (g_qkv, g_proj, g_up, g_down, g_pool)
+    for shard, full in zip(shards, fulls):
+        full[w.x, w.c, w.z, w.y] = shard[...].astype(BF)
+    total = 4 * rows
+    qkv_all[:, pl.ds(total, qkv_all.shape[1] - total)] = jnp.zeros(
+        (3, qkv_all.shape[1] - total, WIDE), BF
+    )
+    small_got[0] = small_in[...]
+    pl.semaphore_wait(barrier, len(peers))
+    gather = Gather(w, fulls, small, small_in, send, recv)
+
+    small_copies = []
+
+    def small_start(index, part):
+        stage = "zyxc"[index]
+        if stage == "z":
+            made = [
+                remote(small_got.at[0], small_got.at[k], send_small.at[k - 1],
+                       recv_small.at[k - 1], w.dev(z=w.z_at(k)))
+                for k in range(1, w.nz)
+            ]
+        else:
+            base = w.nz + 2 * (index - 1)
+            small_got[base] = part
+            made = [
+                remote(small_got.at[base], small_got.at[base + 1],
+                       send_small.at[w.nz + index - 2], recv_small.at[w.nz + index - 2],
+                       w.partner(stage))
+            ]
+        for copy in made:
+            copy.start()
+        small_copies.append(made)
+
+    def small_wait(index):
+        for copy in small_copies[index]:
+            copy.wait_recv()
+        if index == 0:
+            got = small_got[0].astype(F32)
+            for k in range(1, w.nz):
+                got = got + small_got[k].astype(F32)
+        else:
+            base = w.nz + 2 * (index - 1)
+            got = small_got[base].astype(F32) + small_got[base + 1].astype(F32)
+        return got.astype(BF)
+
+    part = None
+    small_start(0, None)
+    gather.start(0, 0)
+    gather.start(1, 0)
+    gather.start(2, 0)
+    for index in range(4):
+        gather.wait(0, index)
+        if index < 3:
+            gather.start(0, index + 1)
+        part = small_wait(index)
+        if index < 3:
+            small_start(index + 1, part)
+        if index == 0:
+            gather.start(3, 0)
+            gather.start(4, 0)
+        elif index == 1:
+            gather.wait(1, 0)
+            gather.start(1, 1)
+            gather.wait(2, 0)
+            gather.start(2, 1)
+    small[...] = part.astype(F32)
+
+    unit, _ = norm_stats(tokens[...].astype(F32))
+    normed = (unit * small[0:1] + small[1:2]).astype(BF)
+
+    def project(x_of):
+        first = pl.multiple_of(x_of * 2 * WIDE, 2 * WIDE)
+        for n in range(3):
+            weight = g_qkv[:, :, :, :, n, :, pl.ds(first, 2 * WIDE)].reshape(D, 2 * WIDE)
+            both = dot(normed, weight)
+            for c_of in range(2):
+                piece = both[:, c_of * WIDE : (c_of + 1) * WIDE]
+                if n < 2:
+                    piece = piece * turn[0] + swap_halves(piece) * turn[1]
+                    if n == 0:
+                        piece = piece * (LOG2E * HEAD_DIM ** -0.5)
+                chunk[x_of * 2 + c_of, n] = piece.astype(BF)
+
+    mine = pl.ds(pl.multiple_of(w.seq * rows, 16), rows)
+    handed = []
+
+    def hand(seq_to, slot):
+        copy = remote(chunk.at[seq_to], qkv_all.at[:, mine], send_x.at[slot], recv_x.at[slot],
+                      (seq_to, w.batch))
+        copy.start()
+        handed.append(copy)
+
+    project(w.xo)
+    hand(w.xo * 2 + w.c, 0)
+    hand(w.xo * 2 + w.co, 1)
+    project(w.x)
+    hand(w.x * 2 + w.co, 2)
+    qkv_all[:, mine] = chunk[w.seq]
+
+    state = {1: 1, 2: 1, 3: 0, 4: 0}
+    for _ in range(4):
+        for a in range(1, ARRAYS):
+            if state[a] < 4:
+                gather.wait(a, state[a])
+                state[a] += 1
+                if state[a] < 4:
+                    gather.start(a, state[a])
+    for copy in handed:
+        copy.wait()
+    for made in small_copies:
+        for copy in made:
+            copy.wait_send()
+    gather.finish()
+
+
+def build_ext(doc_ref, qkv, ext):
+    lane1 = lax.broadcasted_iota(jnp.int32, (1, WIDE), 1)
+    feat1 = lax.rem(lane1, HEAD_DIM)
+    docs = doc_ref[...]
+    lo = jnp.zeros((1, WIDE), jnp.int32)
+    hi = jnp.zeros((1, WIDE), jnp.int32)
+    for d in range(7):
+        below = jnp.sum(jnp.where(docs < d, 1, 0), axis=1, keepdims=True)
+        upto = jnp.sum(jnp.where(docs <= d, 1, 0), axis=1, keepdims=True)
+        lo = jnp.where(feat1 == d, below, lo)
+        hi = jnp.where(feat1 == d, upto, hi)
+    padded = qkv.shape[1]
+    step = 512
+
+    def body(n, _):
+        r0 = pl.multiple_of(n * step, step)
+        rows = lax.broadcasted_iota(jnp.int32, (step, WIDE), 0) + r0
+        lane = lax.broadcasted_iota(jnp.int32, (step, WIDE), 1)
+        feat = lax.rem(lane, HEAD_DIM)
+        same = (rows >= lo) & (rows < hi)
+        q_feat = jnp.where(same, 1.0, 0.0)
+        k_feat = jnp.where(same, 0.0, masked_score)
+        ones = jnp.where((feat >= 8) & (feat < 11), 1.0, 0.0)
+        k_feat = jnp.where(feat < 7, k_feat, ones)
+        parts = [qkv[m, pl.ds(r0, step)].astype(F32) for m in range(3)]
+        for h in range(2):
+            mine = (lane >= h * HEAD_DIM) & (lane < (h + 1) * HEAD_DIM)
+            for m, feats in enumerate((q_feat, k_feat, 1.0)):
+                ext[m, h, pl.ds(r0, step)] = jnp.where(mine, parts[m], feats).astype(BF)
+        return 0
+
+    lax.fori_loop(0, padded // step, body, 0)
+
+
+def with_feats(base, lane, h, vector):
+    one = vector.astype(BF).astype(F32)
+    two = (vector - one).astype(BF).astype(F32)
+    first = (1 - h) * HEAD_DIM + 8
+    for n, term in enumerate((one, two, vector - one - two)):
+        base = jnp.where(lane == first + n, term, base)
+    return base
+
+
+def attend_rows(ext, o_ref, o_low, i, size):
+    padded = ext.shape[2]
+    r0 = i * size
+    n = min(padded, -(-(r0 + size) // 256) * 256)
+    m0 = (r0 // 128) * 128
+    lane = lax.broadcasted_iota(jnp.int32, (size, WIDE), 1)
+    outs = []
+    for h in range(2):
+        q = ext[0, h, pl.ds(r0, size)]
+        s = dot(q, ext[1, h, :n], NT)
+        rows = lax.broadcasted_iota(jnp.int32, (size, n - m0), 0) + r0
+        cols = lax.broadcasted_iota(jnp.int32, (size, n - m0), 1) + m0
+        tail = jnp.where(cols <= rows, s[:, m0:], masked_score)
+        s = jnp.concatenate([s[:, :m0], tail], axis=1) if m0 else tail
+        top = jnp.max(s, axis=1, keepdims=True)
+        p = jnp.exp2(s - top).astype(BF)
+        sums = dot(p, ext[2, h, :n])
+        outs.append(sums / pltpu.roll(sums, HEAD_DIM, 1))
+        log_total = top + jnp.log2(sums)
+        ext[0, h, pl.ds(r0, size)] = with_feats(q.astype(F32), lane, h, -log_total).astype(BF)
+    both = jnp.where(lane < HEAD_DIM, outs[0], outs[1])
+    o_ref[pl.ds(r0, size)] = both
+    o_low[pl.ds(r0, size)] = both.astype(BF)
+
+
+def forward_kernel(doc_ref, qkv_all, ext, o_ref, o_low):
+    total = o_ref.shape[0]
+    build_ext(doc_ref, qkv_all, ext)
+    size = total // 8
+    for i in range(8):
+        attend_rows(ext, o_ref, o_low, i, size)
+    for h in range(2):
+        ext[0, h, pl.ds(total, ext.shape[2] - total)] = jnp.zeros(
+            (ext.shape[2] - total, WIDE), BF
+        )
+
+
+def backward_prep(o_ref, do_ref, do_ext):
+    total = o_ref.shape[0]
+    step = total // 12
+
+    def body(n, _):
+        r0 = pl.multiple_of(n * step, 16)
+        lane = lax.broadcasted_iota(jnp.int32, (step, WIDE), 1)
+        grad = do_ref[pl.ds(r0, step)].astype(F32)
+        terms = grad * o_ref[pl.ds(r0, step)]
+        for h in range(2):
+            mine = (lane >= h * HEAD_DIM) & (lane < (h + 1) * HEAD_DIM)
+            delta = jnp.sum(jnp.where(mine, terms, 0.0), axis=1, keepdims=True)
+            base = jnp.where(mine, grad, 0.0)
+            do_ext[h, pl.ds(r0, step)] = with_feats(base, lane, h, -delta).astype(BF)
+        return 0
+
+    lax.fori_loop(0, 12, body, 0)
+    for h in range(2):
+        do_ext[h, pl.ds(total, do_ext.shape[1] - total)] = jnp.zeros(
+            (do_ext.shape[1] - total, WIDE), BF
+        )
+
+
+def backward_pair(ext, do_ext, dq, dk, dv, h, i, j, size, on_diagonal):
+    ri = pl.multiple_of(i * size, size)
+    rj = pl.multiple_of(j * size, size)
+    q = ext[0, h, pl.ds(ri, size)]
+    k = ext[1, h, pl.ds(rj, size)]
+    v = ext[2, h, pl.ds(rj, size)]
+    grad = do_ext[h, pl.ds(ri, size)]
+    p = jnp.exp2(dot(k, q, NT))
+    if on_diagonal:
+        keys = lax.broadcasted_iota(jnp.int32, (size, size), 0)
+        queries = lax.broadcasted_iota(jnp.int32, (size, size), 1)
+        p = jnp.where(keys <= queries, p, 0.0)
+    ds = (p * dot(v, grad, NT)).astype(BF)
+    p_low = p.astype(BF)
+    if on_diagonal:
+        dv[h, pl.ds(rj, size)] = dot(p_low, grad)
+        dk[h, pl.ds(rj, size)] = dot(ds, q)
+    else:
+        dv[h, pl.ds(rj, size)] += dot(p_low, grad)
+        dk[h, pl.ds(rj, size)] += dot(ds, q)
+    dq[h, pl.ds(ri, size)] += dot(ds, k, TN)
+
+
+def backward_kernel(ext, o_ref, do_ref, out, do_ext, dq, dk, dv):
+    total = o_ref.shape[0]
+    size = 512
+    blocks = ext.shape[2] // size
+    backward_prep(o_ref, do_ref, do_ext)
+    dq[...] = jnp.zeros(dq.shape, F32)
+
+    def per_head(h, _):
+        def per_key(j, _):
+            backward_pair(ext, do_ext, dq, dk, dv, h, j, j, size, True)
+
+            def per_query(i, _):
+                backward_pair(ext, do_ext, dq, dk, dv, h, i, j, size, False)
+                return 0
+
+            lax.fori_loop(j + 1, blocks, per_query, 0)
+            return 0
+
+        lax.fori_loop(0, blocks, per_key, 0)
+        return 0
+
+    lax.fori_loop(0, 2, per_head, 0)
+    step = total // 4
+    scales = (HEAD_DIM ** -0.5, 1.0 / LOG2E, 1.0)
+    for n in range(4):
+        rows = pl.ds(n * step, step)
+        lane = lax.broadcasted_iota(jnp.int32, (step, WIDE), 1)
+        for m, part in enumerate((dq, dk, dv)):
+            both = jnp.where(lane < HEAD_DIM, part[0, rows], part[1, rows])
+            out[n, m] = (both * scales[m]).astype(BF)
+
+
+def middle_kernel(nx, nz, ny, o_low, tokens, out_grad, g_proj, g_up, g_down, g_pool, small,
+                  do_all, short_out, att, normed_two, act, d_hidden, d_branch, d_attn, grouped,
+                  dh_one, small_grad,
+                  dh_two, h_two, h_one, sum_one, sum_two, do_send, next_grad, prev_rows, edge,
+                  send, recv, send_do, recv_do, send_edge, recv_edge):
+    w = Where(nx, nz, ny)
+    rows = tokens.shape[0]
+    pools = rows // 3
+    count = 2 * w.nx
+    peers = w.seq_peers()
+    barrier = greet(peers)
+    first, last = w.seq == 0, w.seq == count - 1
+    g_low = out_grad[...]
+    pool = g_pool[...].reshape(3 * D, D)
+    edge[0] = g_low[0:16]
+    pl.semaphore_wait(barrier, len(peers))
+    grad_edge = remote(edge.at[0], next_grad, send_edge.at[0], recv_edge.at[0],
+                       (w.seq_at(count - 1), w.batch))
+    grad_edge.start()
+    copies = []
+    for k in range(1, count):
+        to = w.seq_at(k)
+        copy = remote(o_low.at[pl.ds(pl.multiple_of(to * rows, 16), rows)], att.at[w.seq],
+                      send.at[k - 1], recv.at[k - 1], (to, w.batch))
+        copy.start()
+        copies.append(copy)
+    att[w.seq] = o_low[pl.ds(pl.multiple_of(w.seq * rows, 16), rows)]
+
+    spread = dot(g_low, pool, NT)
+    tiles = D // WIDE
+
+    def lay(ref, start, value):
+        for n in range(tiles):
+            ref[n, pl.ds(start, value.shape[0])] = value[:, n * WIDE : (n + 1) * WIDE]
+
+    def whole(ref):
+        return jnp.concatenate([ref[n, pl.ds(8, rows)] for n in range(tiles)], axis=1)
+
+    for k in range(3):
+        for n in range(tiles):
+            at = k * D + n * WIDE
+            dh_two[n, pl.ds(6 + k, pools, stride=3)] = spread[:, at : at + WIDE]
+    grad_edge.wait()
+    beyond = dot(next_grad[...], pool, NT)
+    beyond = jnp.where(last, 0.0, beyond)
+    lay(dh_two, 8 + rows - 2, beyond[0:1, 0:D])
+    lay(dh_two, 8 + rows - 1, beyond[0:1, D : 2 * D])
+    d_branch[...] = whole(dh_two).astype(BF)
+    small_grad[...] = jnp.zeros(small_grad.shape, F32)
+    small_grad[4:5] = jnp.sum(d_branch[...].astype(F32), axis=0, keepdims=True)
+    small_grad[5:6] = jnp.sum(g_low.astype(F32), axis=0, keepdims=True)
+
+    for copy in copies:
+        copy.wait()
+    attended = jnp.concatenate([att[n] for n in range(count)], axis=1)
+    h_one[...] = tokens[...].astype(F32) + dot(attended, g_proj[...].reshape(D, D))
+    unit, _ = norm_stats(h_one[...])
+    normed_two[...] = (unit * small[2:3] + small[3:4]).astype(BF)
+    sum_one[...] = jnp.zeros(sum_one.shape, F32)
+    sum_two[...] = jnp.zeros(sum_two.shape, F32)
+    part = act.shape[1] // count
+
+    def feed(n, _):
+        cols = pl.ds(pl.multiple_of(n * part, part), part)
+        up = g_up[:, :, :, :, :, cols].reshape(D, part)
+        down = g_down[lax.div(n, 2), lax.rem(n, 2)].reshape(part, D)
+        hidden = dot(normed_two[...], up) + small[pl.ds(6 + n, 1)]
+        square = hidden * hidden
+        bend = jnp.tanh(GELU_C * hidden * (1.0 + 0.044715 * square))
+        half = 0.5 * (1.0 + bend)
+        act_low = (hidden * half).astype(BF)
+        act[:, cols] = act_low
+        slope = half + 0.5 * hidden * (1.0 - bend * bend) * (
+            GELU_C * (1.0 + 3 * 0.044715 * square)
+        )
+        sum_one[...] += dot(act_low, down)
+        d_low = (dot(d_branch[...], down, NT) * slope).astype(BF)
+        d_hidden[:, cols] = d_low
+        small_grad[pl.ds(6 + n, 1)] = jnp.sum(d_low.astype(F32), axis=0, keepdims=True)
+        sum_two[...] += dot(d_low, up, NT)
+        return 0
+
+    lax.fori_loop(0, count, feed, 0)
+    h_low = (h_one[...] + sum_one[...] + small[4:5]).astype(BF)
+    lay(h_two, 8, h_low.astype(F32))
+    edge[1] = h_low[rows - 16 :]
+    row_edge = remote(edge.at[1], prev_rows, send_edge.at[1], recv_edge.at[1],
+                      (w.seq_at(1), w.batch))
+    row_edge.start()
+    unit, scale = norm_stats(h_one[...])
+    back, small_grad[2:3], small_grad[3:4] = norm_back(sum_two[...], unit, scale, small[2:3])
+    grad_one = whole(dh_two) + back
+    dh_one[...] = grad_one
+    d_attn[...] = grad_one.astype(BF)
+    spread_back = dot(d_attn[...], g_proj[...].reshape(D, D), NT).astype(BF)
+    for n in range(count):
+        do_send[n] = spread_back[:, n * WIDE : (n + 1) * WIDE]
+    mine = pl.ds(pl.multiple_of(w.seq * rows, 16), rows)
+    given = []
+    for k in range(1, count):
+        to = w.seq_at(k)
+        copy = remote(do_send.at[to], do_all.at[mine], send_do.at[k - 1], recv_do.at[k - 1],
+                      (to, w.batch))
+        copy.start()
+        given.append(copy)
+    do_all[mine] = do_send[w.seq]
+
+    row_edge.wait()
+    before = jnp.where(first, 0.0, prev_rows[...].astype(F32))
+    lay(h_two, 0, before[8:16])
+    for k in range(3):
+        for n in range(tiles):
+            at = k * D + n * WIDE
+            grouped[:, at : at + WIDE] = h_two[n, pl.ds(6 + k, pools, stride=3)].astype(BF)
+    short_out[...] = (dot(grouped[...], pool) + small[5:6]).astype(BF)
+    for copy in given:
+        copy.wait()
+
+
+class Scatter:
+    ORDERS = ("xy", "yx", "yx", "xy", "yx")
+
+    def __init__(self, w, acc, c_out, c_in, two_out, two_in, three_out, three_in, z_out, z_in,
+                 send, recv):
+        self.w, self.acc = w, acc
+        self.c_out, self.c_in = c_out, c_in
+        self.two_out, self.two_in = two_out, two_in
+        self.three_out, self.three_in = three_out, three_in
+        self.z_out, self.z_in = z_out, z_in
+        self.send, self.recv = send, recv
+        self.copies = {}
+
+    def go(self, a, index, src, dst, slot, peer):
+        copy = remote(src, dst, self.send.at[a, slot], self.recv.at[a, slot], peer)
+        copy.start()
+        self.copies.setdefault((a, index), []).append(copy)
+
+    def arrived(self, a, index):
+        for copy in self.copies[a, index]:
+            copy.wait_recv()
+
+    def begin(self, a, make):
+        w = self.w
+        shape = self.acc[a].shape[1:]
+        for x_of in range(w.nx):
+            self.c_out[a][x_of] = make(x_of * 2 + w.co).reshape(shape).astype(BF)
+        self.go(a, 0, self.c_out[a], self.c_in[a], 0, w.partner("c"))
+        for x_of in range(w.nx):
+            self.acc[a][x_of] = make(x_of * 2 + w.c).reshape(shape)
+
+    def step_two(self, a):
+        w = self.w
+        acc, got, out = self.acc[a], self.c_in[a], self.two_out[a]
+        self.arrived(a, 0)
+        by_x = self.ORDERS[a][0] == "x"
+
+        def body(n, _):
+            if by_x:
+                out[n] = (acc[w.xo, n] + got[w.xo, n].astype(F32)).astype(BF)
+            else:
+                for x_of in range(w.nx):
+                    out[x_of, n] = (acc[x_of, n, w.yo] + got[x_of, n, w.yo].astype(F32)).astype(BF)
+            return 0
+
+        lax.fori_loop(0, w.nz, body, 0)
+        self.go(a, 1, out, self.two_in[a], 1, w.partner(self.ORDERS[a][0]))
+
+    def step_three(self, a):
+        w = self.w
+        acc, got, more, out = self.acc[a], self.c_in[a], self.two_in[a], self.three_out[a]
+        self.arrived(a, 1)
+        by_x = self.ORDERS[a][0] == "x"
+
+        def body(n, _):
+            if by_x:
+                out[n] = (acc[w.x, n, w.yo] + got[w.x, n, w.yo].astype(F32)
+                          + more[n, w.yo].astype(F32)).astype(BF)
+                acc[w.x, n, w.y] = (acc[w.x, n, w.y] + got[w.x, n, w.y].astype(F32)
+                                    + more[n, w.y].astype(F32))
+            else:
+                out[n] = (acc[w.xo, n, w.y] + got[w.xo, n, w.y].astype(F32)
+                          + more[w.xo, n].astype(F32)).astype(BF)
+                acc[w.x, n, w.y] = (acc[w.x, n, w.y] + got[w.x, n, w.y].astype(F32)
+                                    + more[w.x, n].astype(F32))
+            return 0
+
+        lax.fori_loop(0, w.nz, body, 0)
+        self.go(a, 2, out, self.three_in[a], 2, w.partner(self.ORDERS[a][1]))
+
+    def step_four(self, a):
+        w = self.w
+        acc, more = self.acc[a], self.three_in[a]
+        self.arrived(a, 2)
+        for k in range(1, w.nz):
+            to = w.z_at(k)
+            self.z_out[a][k - 1] = (acc[w.x, to, w.y] + more[to].astype(F32)).astype(BF)
+            self.go(a, 3, self.z_out[a].at[k - 1], self.z_in[a].at[k - 1], 2 + k, w.dev(z=to))
+        acc[w.x, w.z, w.y] = acc[w.x, w.z, w.y] + more[w.z].astype(F32)
+
+    def last(self, a):
+        w = self.w
+        self.arrived(a, 3)
+        total = self.acc[a][w.x, w.z, w.y]
+        for k in range(1, w.nz):
+            total = total + self.z_in[a][k - 1].astype(F32)
+        return total
+
+    def finish(self):
+        for made in self.copies.values():
+            for copy in made:
+                copy.wait_send()
+
+
+def end_kernel(nx, nz, ny, *refs):
+    (d_qkv, tokens, turn, g_qkv, small, att, normed_two, act, d_hidden, d_branch, d_attn,
+     grouped, out_grad, dh_one, small_grad) = refs[:15]
+    states = refs[15:30]
+    (input_grad, small_total, norm_out) = refs[30:33]
+    new_states = refs[33:48]
+    scratch = list(refs[48:])
+    take = lambda n: tuple(scratch.pop(0) for _ in range(n))
+    back_in, stacked, normed = take(3)
+    groups = [take(ARRAYS) for _ in range(9)]
+    small_got, norm_got = take(2)
+    send, recv, send_x, recv_x, send_small, recv_small, send_norm, recv_norm = take(8)
+
+    w = Where(nx, nz, ny)
+    rows = tokens.shape[0]
+    count = 2 * w.nx
+    others = [(w.seq, lax.rem(w.batch + k, w.nz * w.ny)) for k in range(1, w.nz * w.ny)]
+    peers = w.seq_peers() + others
+    barrier = greet(peers)
+    pl.semaphore_wait(barrier, len(peers))
+
+    handed = []
+    for k in range(1, count):
+        to = w.seq_at(k)
+        copy = remote(d_qkv.at[to], back_in.at[w.seq], send_x.at[k - 1], recv_x.at[k - 1],
+                      (to, w.batch))
+        copy.start()
+        handed.append(copy)
+    back_in[w.seq] = d_qkv[w.seq]
+
+    scatter = Scatter(w, *groups, send, recv)
+
+    def columns(ref):
+        width = ref.shape[1] // count
+        return lambda block: ref[:, pl.ds(pl.multiple_of(block * width, WIDE), width)]
+
+    lhs_down, lhs_pool = columns(act), columns(grouped)
+    lhs_up, lhs_qkv = columns(normed_two), columns(normed)
+    scatter.begin(3, lambda block: dot(lhs_down(block), d_branch[...], TN))
+    scatter.begin(2, lambda block: dot(lhs_up(block), d_hidden[...], TN))
+    scatter.step_two(3)
+    scatter.begin(4, lambda block: dot(lhs_pool(block), out_grad[...], TN))
+    scatter.step_two(2)
+    scatter.begin(1, lambda block: dot(att[block], d_attn[...], TN))
+    scatter.step_two(4)
+    scatter.step_two(1)
+
+    for copy in handed:
+        copy.wait()
+    unit, scale = norm_stats(tokens[...].astype(F32))
+    normed[...] = (unit * small[0:1] + small[1:2]).astype(BF)
+    for n in range(3):
+        for b in range(count):
+            piece = back_in[b, n]
+            if n < 2:
+                piece = piece.astype(F32)
+                piece = (piece * turn[0] - swap_halves(piece) * turn[1]).astype(BF)
+            stacked[n, :, b * WIDE : (b + 1) * WIDE] = piece
+
+    def grad_qkv(block):
+        left = lhs_qkv(block)
+        parts = [dot(left, stacked[n], TN).reshape(w.nz, w.ny, 1, -1, D) for n in range(3)]
+        return jnp.concatenate(parts, axis=2)
+
+    scatter.begin(0, grad_qkv)
+    scatter.step_two(0)
+    grad_normed = sum(dot(stacked[n], g_qkv[:, :, :, :, n].reshape(D, D), NT) for n in range(3))
+    back, small_grad[0:1], small_grad[1:2] = norm_back(grad_normed, unit, scale, small[0:1])
+    input_grad[...] = dh_one[...] + back
+
+    small_copies = []
+    small_got[0] = small_grad[...]
+    for index, stage in enumerate("cyx"):
+        copy = remote(small_got.at[2 * index], small_got.at[2 * index + 1],
+                      send_small.at[index], recv_small.at[index], w.partner(stage))
+        copy.start()
+        small_copies.append(copy)
+        if index == 0:
+            for a in (3, 2, 4, 1):
+                scatter.step_three(a)
+        elif index == 1:
+            scatter.step_three(0)
+            scatter.step_four(3)
+            scatter.step_four(2)
+        copy.wait_recv()
+        small_got[2 * index + 2] = small_got[2 * index] + small_got[2 * index + 1]
+    z_first = 7
+    for k in range(1, w.nz):
+        copy = remote(small_got.at[6], small_got.at[z_first + w.z], send_small.at[2 + k],
+                      recv_small.at[2 + k], w.dev(z=w.z_at(k)))
+        copy.start()
+        small_copies.append(copy)
+    small_got[z_first + w.z] = small_got[6]
+    for a in (4, 1, 0):
+        scatter.step_four(a)
+    for copy in small_copies[3:]:
+        copy.wait_recv()
+    whole = small_got[z_first]
+    for k in range(1, w.nz):
+        whole = whole + small_got[z_first + k]
+    small_total[...] = whole
+
+    totals = {}
+    squares = jnp.zeros((8, D), F32)
+    for a in range(ARRAYS):
+        total = scatter.last(a)
+        totals[a] = total
+        width = total.shape[-1]
+        flat = (total * total).reshape(-1, 8, width)
+        flat = jnp.sum(flat, axis=0)
+        for n in range(width // D):
+            squares = squares + flat[:, n * D : (n + 1) * D]
+        scatter.acc[a][w.x, w.z, w.y] = total
+    squares = sum(squares[:, n * WIDE : (n + 1) * WIDE] for n in range(D // WIDE))
+    norm_copies = []
+    norm_got[w.seq] = squares
+    for k in range(1, count):
+        copy = remote(norm_got.at[w.seq], norm_got.at[w.seq], send_norm.at[k - 1],
+                      recv_norm.at[k - 1], (w.seq_at(k), w.batch))
+        copy.start()
+        norm_copies.append(copy)
+    for copy in norm_copies:
+        copy.wait_recv()
+    part = norm_got[0]
+    for n in range(1, count):
+        part = part + norm_got[n]
+    here = count + w.batch
+    norm_got[here] = part
+    for k, peer in enumerate(others):
+        copy = remote(norm_got.at[here], norm_got.at[here], send_norm.at[count - 1 + k],
+                      recv_norm.at[count - 1 + k], peer)
+        copy.start()
+        norm_copies.append(copy)
+    for copy in norm_copies[count - 1 :]:
+        copy.wait_recv()
+    part = norm_got[count]
+    for n in range(1, w.nz * w.ny):
+        part = part + norm_got[count + n]
+    square = jnp.sum(jnp.sum(part, axis=1, keepdims=True), axis=0, keepdims=True)
+    extra = jnp.sum(jnp.sum(whole * whole, axis=1, keepdims=True), axis=0, keepdims=True)
+    grad_norm = jnp.sqrt(square + extra)
+    norm_out[...] = jnp.broadcast_to(grad_norm, norm_out.shape)
+    clip = clip_norm / jnp.maximum(grad_norm, clip_norm)
+    for a in range(ARRAYS):
+        weight, one, two = states[3 * a : 3 * a + 3]
+        total = scatter.acc[a][w.x, w.z, w.y]
+        limit = clip.reshape((1,) * total.ndim)
+        results = adam_update(total, one[...], two[...], weight[...], limit, rate_matrix,
+                              decay_weight)
+        for ref, value in zip(new_states[3 * a : 3 * a + 3], results):
+            ref[...] = value
+    for copy in small_copies + norm_copies:
+        copy.wait_send()
+    scatter.finish()
+
+
+def fast_local(mesh):
+    nx, nz, ny = grid_of(mesh)
+    count = 2 * nx
+    whole_mem = pl.BlockSpec(memory_space=pltpu.VMEM)
+    dma = lambda *shape: pltpu.SemaphoreType.DMA(shape)
+
+    def call(kernel, outs, scratch, args, collective=None):
+        params = dict(vmem_limit_bytes=VMEM_LIMIT)
+        if collective is not None:
+            params.update(collective_id=collective, has_side_effects=True)
+        return pl.pallas_call(
+            kernel,
+            out_shape=[jax.ShapeDtypeStruct(s, t) for s, t in outs],
+            in_specs=[whole_mem] * len(args),
+            out_specs=[whole_mem] * len(outs),
+            scratch_shapes=scratch,
+            compiler_params=pltpu.CompilerParams(**params),
+        )(*args)
+
+    def body(tokens, doc_ids, out_grad,
+             qkv_weight, qkv_first, qkv_second,
+             proj_weight, proj_first, proj_second,
+             up_weight, up_first, up_second,
+             down_weight, down_first, down_second,
+             pool_weight, pool_first, pool_second,
+             small_weight, small_first, small_second):
+        rows = tokens.shape[1]
+        total = rows * count
+        padded = -(-total // 512) * 512
+        pools = out_grad.shape[1]
+        ff = up_weight.shape[1]
+        tok = tokens[0]
+        grad = out_grad[0]
+        seq, batch = lax.axis_index("seq"), lax.axis_index("batch")
+        shard = seq * (nz * ny) + batch
+        own = small_weight.shape[0]
+        small_len = own * count * nz * ny
+        place = lax.dynamic_update_slice(
+            jnp.zeros((16 * D,), BF), small_weight.astype(BF), (shard * own,)
+        ).reshape(16, D)
+        half = HEAD_DIM // 2
+        lanes = jnp.arange(WIDE)
+        frequency = jnp.exp(-math.log(10000.0) * jnp.arange(half, dtype=F32) / half)
+        positions = seq * rows + jnp.arange(rows, dtype=jnp.int32)
+        angles = positions.astype(F32)[:, None] * frequency[None, :]
+        cosine, sine = jnp.cos(angles), jnp.sin(angles)
+        turn = jnp.stack([
+            jnp.concatenate([cosine] * 4, axis=1),
+            jnp.concatenate([-sine, sine] * 2, axis=1),
+        ])
+        weights = (qkv_weight, proj_weight, up_weight, down_weight, pool_weight)
+        firsts = (qkv_first, proj_first, up_first, down_first, pool_first)
+        seconds = (qkv_second, proj_second, up_second, down_second, pool_second)
+        lead = (nx, 2, nz, ny)
+        outs = [(lead + v.shape, BF) for v in weights]
+        outs += [((16, D), F32), ((3, padded, WIDE), BF)]
+        *fulls, small, qkv_all = call(
+            lambda *r: start_kernel(nx, nz, ny, *r), outs,
+            [pltpu.VMEM((count, 3, rows, WIDE), BF), pltpu.VMEM((nz + 6, 16, D), BF),
+             dma(ARRAYS, nz + 2), dma(ARRAYS, nz + 2), dma(nz + 2), dma(nz + 2), dma(3), dma(3)],
+            (tok, *weights, place, turn), 0)
+        g_qkv, g_proj, g_up, g_down, g_pool = fulls
+        ext, o_ref, o_low = call(
+            forward_kernel,
+            [((3, 2, padded, WIDE), BF), ((total, WIDE), F32), ((total, WIDE), BF)], [],
+            (doc_ids, qkv_all))
+        outs = [((total, WIDE), BF), ((pools, D), BF), ((count, rows, WIDE), BF),
+                ((rows, D), BF), ((rows, ff), BF), ((rows, ff), BF), ((rows, D), BF),
+                ((rows, D), BF), ((pools, 3 * D), BF), ((rows, D), F32), ((16, D), F32)]
+        (do_all, short_out, att, normed_two, act, d_hidden, d_branch, d_attn, grouped, dh_one,
+         small_grad) = call(
+            lambda *r: middle_kernel(nx, nz, ny, *r), outs,
+            [pltpu.VMEM((D // WIDE, rows + 16, WIDE), F32),
+             pltpu.VMEM((D // WIDE, rows + 16, WIDE), F32),
+             pltpu.VMEM((rows, D), F32), pltpu.VMEM((rows, D), F32), pltpu.VMEM((rows, D), F32),
+             pltpu.VMEM((count, rows, WIDE), BF), pltpu.VMEM((16, D), BF),
+             pltpu.VMEM((16, D), BF), pltpu.VMEM((2, 16, D), BF),
+             dma(3), dma(3), dma(3), dma(3), dma(2), dma(2)],
+            (o_low, tok, grad, g_proj, g_up, g_down, g_pool, small), 1)
+        (d_qkv,) = call(
+            backward_kernel, [((count, 3, rows, WIDE), BF)],
+            [pltpu.VMEM((2, padded, WIDE), BF)] + [pltpu.VMEM((2, padded, WIDE), F32)] * 3,
+            (ext, o_ref, do_all))
+
+        shapes = [v.shape for v in weights]
+        outs = [((rows, D), F32), ((16, D), F32), ((8, WIDE), F32)]
+        outs += [(s, F32) for s in shapes for _ in range(3)]
+        scratch = [pltpu.VMEM((count, 3, rows, WIDE), BF), pltpu.VMEM((3, rows, D), BF),
+                   pltpu.VMEM((rows, D), BF)]
+        scratch += [pltpu.VMEM((nx, nz, ny) + s, F32) for s in shapes]
+        scratch += [pltpu.VMEM((nx, nz, ny) + s, BF) for _ in range(2) for s in shapes]
+        two = [(nz, ny) if o[0] == "x" else (nx, nz) for o in Scatter.ORDERS]
+        scratch += [pltpu.VMEM(t + s, BF) for _ in range(2) for t, s in zip(two, shapes)]
+        scratch += [pltpu.VMEM((nz,) + s, BF) for _ in range(2) for s in shapes]
+        scratch += [pltpu.VMEM((nz - 1,) + s, BF) for _ in range(2) for s in shapes]
+        scratch += [pltpu.VMEM((7 + nz, 16, D), F32),
+                    pltpu.VMEM((count + nz * ny, 8, WIDE), F32)]
+        norm_slots = count - 1 + nz * ny - 1
+        for slots in ((ARRAYS, nz + 2), (3,), (nz + 2,), (norm_slots,)):
+            scratch += [dma(*slots), dma(*slots)]
+        states = [v for trio in zip(weights, firsts, seconds) for v in trio]
+        done = call(
+            lambda *r: end_kernel(nx, nz, ny, *r), outs, scratch,
+            (d_qkv, tok, turn, g_qkv, small, att, normed_two, act, d_hidden, d_branch, d_attn,
+             grouped, grad, dh_one, small_grad, *states), 2)
+        input_grad, small_total, norm_out = done[:3]
+        new_states = done[3:]
+        grad_norm = norm_out[0, 0]
+        clip = clip_norm / jnp.maximum(grad_norm, clip_norm)
+        small_part = lax.dynamic_slice(small_total.reshape(-1), (shard * own,), (own,))
+        small_new = adam_update(small_part, small_first, small_second, small_weight, clip,
+                                rate_vector, 0.0)
+        return (short_out[None], input_grad[None], grad_norm, *new_states, *small_new)
+
+    return body
+
+
 def solution(mesh):
     in_specs = (
         P("batch", "seq", None),
@@ -406,4 +1327,5 @@
         P(("seq", "batch")),
         P(("seq", "batch")),
     )
-    return jax.shard_map(local, mesh=mesh, in_specs=in_specs, out_specs=out_specs, check_vma=False)
+    body = fast_local(mesh) if fits(mesh) else local
+    return jax.shard_map(body, mesh=mesh, in_specs=in_specs, out_specs=out_specs, check_vma=False)

time: 1310 us -> 286 us (0.22)
  waiting for transfers between devices: 631 us -> 0 us
  Pallas kernels: 0 us -> 262 us
  matrix products: 230 us -> 0 us
  blocking collectives: 198 us -> 0 us
  other arithmetic: 134 us -> 4.01 us
  local copies, waits for them, and re-layouts: 83.9 us -> 15.8 us
  between operations: 21 us -> 1.52 us
    reduce_scatter x5 -> x0, waiting for transfers between devices: 491 us -> none  [the longest x1 142 us: local(): lax.psum_scatter(all_grads[3], ('seq', 'batch'), scatter_dimension=0, til...]
    pallas_call x0 -> x5, Pallas kernels: none -> 262 us  [call(): pl.pallas_call(kernel, out_shape=[jax.ShapeDtypeStruct(s, t) for s, t in...]
    dot_general x39 -> x0, matrix products: 230 us -> none  [the longest x3 50.4 us: block_first(): jnp.einsum('qhd,khd->hqk', grad_heads, value_heads, preferred_element_typ...]
    unnamed x15 -> x0, waiting for transfers between devices: 89.7 us -> none
    unnamed x2 -> x0, blocking collectives: 82.4 us -> none
    all_gather x1 -> x0, blocking collectives: 71.2 us -> none  [local(): lax.all_gather(proj_weight.astype(jnp.bfloat16), ('seq', 'batch'), axis=0...]
    convert_element_type x10 -> x2, other arithmetic: 58.3 us -> 0.69 us  [the longest x1 0.68 us: body(): small_weight.astype(BF)]
    reduce_sum x17 -> x0, other arithmetic: 52.3 us -> none  [the longest x4 37.1 us: block_stats(): return (block_max, jnp.sum(jnp.exp(scores - block_max[..., None]), axis=-1))]
  transfers between devices with their start and end apart: 15 -> 0, of which waited for: 8 -> 0; matrix products, arithmetic and copies ran while one was open for 21% -> 0% of each run, Pallas kernels for 0% -> 0%
where the time goes in v1:
time: 286 us; the launch traced here: 283 us
  Pallas kernels  262 us (92%)
  local copies, waits for them, and re-layouts  15.8 us (6%)
  other arithmetic  4.01 us (1%)
    pallas_call x5, Pallas kernels, call(): pl.pallas_call(kernel, out_shape=[jax.ShapeDtypeStruct(s, t) for s, t in...  262 us
    unnamed x56, local copies, waits for them, and re-layouts  13.7 us

profile of v1, /device:TPU:12, one launch (start us, length us, event | category | flops | bytes accessed | tf_op | source)
XLA Modules:
  0.0 283.0 jit_solution(5318489285849598510)
XLA Ops:
  0.7 0.7 convert_element_type.10
  2.3 1.2 multiply_cosine_fusion
  4.0 0.9 pad_maximum_fusion.r_7_.r_2_
  4.9 93.3 %shard_map.364 = (bf16[2,2,4,2,3,16,512]{6,5,4,3,2,1,0:T(8,128)(2,1)}, bf16[2,2,4,2,16,512]{5,4,3,2,1,0:T(8,128)(2,1)}, bf16[2,2,4,2,16,2048]{5,4,3,2,1,0:T(8,12...) custom-call(bf16[624,512]{1,0:T(8,128)(2,1)} %bitcast.11, ...), custom_call_target="tpu_custom_call" | custom-call | tf_op jit(solution)/shard_map/pallas_call | solution.py:1176
  98.3 16.3 %shard_map.365 = (bf16[3,2,2560,128]{3,2,1,0:T(8,128)(2,1)}, f32[2496,128]{1,0:T(8,128)}, bf16[2496,128]{1,0:T(8,128)(2,1)}) custom-call(s32[1,2496]{1,0:T(1,128)} %doc_ref.1, bf16[3,2560,128]{2,1,0:T(8,128)(2,1)} %get-tuple-element.60.qkv_all), custom_call_target="tpu_custom_call" | custom-call | tf_op jit(solution)/shard_map/pallas_call | solution.py:1176
  114.6 34.2 %shard_map.366 = (bf16[2496,128]{1,0:T(8,128)(2,1)}, bf16[208,512]{1,0:T(8,128)(2,1)}, bf16[4,624,128]{2,1,0:T(8,128)(2,1)}, bf16[624,512]{1,0:T(8,128)(2,1)}, b...) custom-call(bf16[2496,128]{1,0:T(8,128)(2,1)} %get-tuple-element.61., ...), custom_call_target="tpu_custom_call" | custom-call | tf_op jit(solution)/shard_map/pallas_call | solution.py:1176
  148.8 31.9 %shard_map.367.r_0_ = bf16[4,3,624,128]{3,2,1,0:T(8,128)(2,1)} custom-call(bf16[3,2,2560,128]{3,2,1,0:T(8,128)(2,1)} %get-tuple-element.68.ext, f32[2496,128]{1,0:T(8,128)} %get-tuple-element.69.o_ref, bf16[2496,128]{1,0:T(8,128)(2,1)} %get-tuple-element.70.do_ref), custom_call_target="tpu_custom_call" | custom-call | tf_op jit(solution)/shard_map/pallas_call | solution.py:1176
  180.6 86.0 %shard_map.368 = (f32[624,512]{1,0:T(8,128)}, f32[16,512]{1,0:T(8,128)}, f32[8,128]{1,0:T(8,128)}, f32[3,16,512]{2,1,0:T(8,128)}, f32[3,16,512]{2,1,0:T(8,128)},...) custom-call(bf16[4,3,624,128]{3,2,1,0:T(8,128)(2,1)} %shard_map.367., ...), custom_call_target="tpu_custom_call" | custom-call | tf_op jit(solution)/shard_map/pallas_call | solution.py:1176
  266.7 1.3 slice.3
  268.7 0.8 copy.43
  269.5 0.7 multiply_subtract_fusion
  270.2 0.7 copy.62
  270.9 2.5 copy.63
  273.4 0.6 copy.64
  274.0 0.6 copy.65
  274.7 0.6 copy.66
  277.2 0.7 copy.70
  277.8 0.7 copy.71
  278.5 0.7 copy.72
  279.1 0.7 copy.73
  279.8 0.7 copy.74
  280.5 0.7 copy.75
  281.1 0.6 copy.76
  281.8 0.6 copy.77
  (48 shorter events, 4.0 us)
Async XLA Ops:
  180.6 88.8 %copy-start.16 = (f32[160]{0:T(256)S(1)}, f32[160]{0:T(256)}, u32[]{:S(2)}) copy-start(f32[160]{0:T(256)} %param.39) | copy-start | bytes 1924
  180.6 88.8 %copy-start.17 = (f32[160]{0:T(256)S(1)}, f32[160]{0:T(256)}, u32[]{:S(2)}) copy-start(f32[160]{0:T(256)} %param.41) | copy-start | bytes 1924
  180.6 88.8 %copy-start.18 = (f32[160]{0:T(256)S(1)}, f32[160]{0:T(256)}, u32[]{:S(2)}) copy-start(f32[160]{0:T(256)} %param.40) | copy-start | bytes 1924
  180.6 89.5 %copy-start = (bf16[208,512]{1,0:T(8,128)(2,1)S(1)}, bf16[208,512]{1,0:T(8,128)(2,1)}, u32[]{:S(2)}) copy-start(bf16[208,512]{1,0:T(8,128)(2,1)} %get-tuple-element.67) | copy-start | bytes 638980
  266.6 6.7 %copy-start.12 = (f32[3,16,512]{2,1,0:T(8,128)S(1)}, f32[3,16,512]{2,1,0:T(8,128)}, u32[]{:S(2)}) copy-start(f32[3,16,512]{2,1,0:T(8,128)} %get-tuple-element.131) | copy-start | bytes 294916
  266.6 7.4 %copy-start.11 = (f32[3,16,512]{2,1,0:T(8,128)S(1)}, f32[3,16,512]{2,1,0:T(8,128)}, u32[]{:S(2)}) copy-start(f32[3,16,512]{2,1,0:T(8,128)} %get-tuple-element.132) | copy-start | bytes 294916
  266.6 8.0 %copy-start.10 = (f32[3,16,512]{2,1,0:T(8,128)S(1)}, f32[3,16,512]{2,1,0:T(8,128)}, u32[]{:S(2)}) copy-start(f32[3,16,512]{2,1,0:T(8,128)} %get-tuple-element.133) | copy-start | bytes 294916
  266.6 8.7 %copy-start.15 = (f32[16,512]{1,0:T(8,128)S(1)}, f32[16,512]{1,0:T(8,128)}, u32[]{:S(2)}) copy-start(f32[16,512]{1,0:T(8,128)} %get-tuple-element.134) | copy-start | bytes 98308
  266.7 9.3 %copy-start.14 = (f32[16,512]{1,0:T(8,128)S(1)}, f32[16,512]{1,0:T(8,128)}, u32[]{:S(2)}) copy-start(f32[16,512]{1,0:T(8,128)} %get-tuple-element.135) | copy-start | bytes 98308
  266.7 9.9 %copy-start.13 = (f32[16,512]{1,0:T(8,128)S(1)}, f32[16,512]{1,0:T(8,128)}, u32[]{:S(2)}) copy-start(f32[16,512]{1,0:T(8,128)} %get-tuple-element.136) | copy-start | bytes 98308
  268.6 8.5 %copy-start.6 = (f32[16,2048]{1,0:T(8,128)S(1)}, f32[16,2048]{1,0:T(8,128)}, u32[]{:S(2)}) copy-start(f32[16,2048]{1,0:T(8,128)} %get-tuple-element.137) | copy-start | bytes 393220
  270.2 7.7 %copy-start.5 = (f32[16,2048]{1,0:T(8,128)S(1)}, f32[16,2048]{1,0:T(8,128)}, u32[]{:S(2)}) copy-start(f32[16,2048]{1,0:T(8,128)} %get-tuple-element.138) | copy-start | bytes 393220
  270.8 7.6 %copy-start.4 = (f32[16,2048]{1,0:T(8,128)S(1)}, f32[16,2048]{1,0:T(8,128)}, u32[]{:S(2)}) copy-start(f32[16,2048]{1,0:T(8,128)} %get-tuple-element.139) | copy-start | bytes 393220
  270.8 8.3 %copy-start.3 = (f32[64,512]{1,0:T(8,128)S(1)}, f32[64,512]{1,0:T(8,128)}, u32[]{:S(2)}) copy-start(f32[64,512]{1,0:T(8,128)} %get-tuple-element.140) | copy-start | bytes 393220
  270.8 8.9 %copy-start.2 = (f32[64,512]{1,0:T(8,128)S(1)}, f32[64,512]{1,0:T(8,128)}, u32[]{:S(2)}) copy-start(f32[64,512]{1,0:T(8,128)} %get-tuple-element.141) | copy-start | bytes 393220
  270.8 9.6 %copy-start.1 = (f32[64,512]{1,0:T(8,128)S(1)}, f32[64,512]{1,0:T(8,128)}, u32[]{:S(2)}) copy-start(f32[64,512]{1,0:T(8,128)} %get-tuple-element.142) | copy-start | bytes 393220
  270.9 10.3 %copy-start.9 = (f32[48,512]{1,0:T(8,128)S(1)}, f32[48,512]{1,0:T(8,128)}, u32[]{:S(2)}) copy-start(f32[48,512]{1,0:T(8,128)} %get-tuple-element.143) | copy-start | bytes 294916
  273.4 8.4 %copy-start.8 = (f32[48,512]{1,0:T(8,128)S(1)}, f32[48,512]{1,0:T(8,128)}, u32[]{:S(2)}) copy-start(f32[48,512]{1,0:T(8,128)} %get-tuple-element.144) | copy-start | bytes 294916
  273.4 9.0 %copy-start.7 = (f32[48,512]{1,0:T(8,128)S(1)}, f32[48,512]{1,0:T(8,128)}, u32[]{:S(2)}) copy-start(f32[48,512]{1,0:T(8,128)} %get-tuple-element.145) | copy-start | bytes 294916
